TPU v7x, 512 devices: a whole 4x4x16 slice. The times are simulated.
512 devices in a mesh: rep: 32 (over y, x, core), tp: 16 (over z).
Axes of the slice: x: 4, y: 4, z: 16, core: 2. Of those that a mesh axis runs over, the one named last changes fastest.
Arguments:
- queries: bfloat16 [1024, 4096], P('rep', 'tp'), may hold values from -110 to 110
- new_key_value: bfloat16 [1024, 16, 256], P('rep', 'tp'), may hold values from -6 to 6
- key_value_cache: bfloat16 [1024, 16, 128, 256], P('rep', 'tp'), may hold values from -4 to 4
- lengths: int32 [1024], P('rep'), may hold values from 2 to 128
- residual: bfloat16 [1024, 4096], P('rep', 'tp'), may hold values from -1.1953125 to 1.1953125
- output_weight: bfloat16 [4096, 4096], P('tp'), may hold values from -0.09375 to 0.09375
- row_adapter_index: int32 [1024], P('rep'), may hold values from 0 to 127, as said below
- adapter_storage_slot: int32 [128], replicated, may hold values from 0 to 127, as said below
- adapter_down_weight: bfloat16 [128, 4096, 64], P('rep', 'tp'), may hold values from -0.09375 to 0.09375
- adapter_up_weight: bfloat16 [128, 64, 4096], P('rep', None, 'tp'), may hold values from -0.75 to 0.75
Outputs:
- layer_out: bfloat16 [1024, 4096], P('rep', 'tp')
Inputs may be any that keep to these rules, and one draw needn't show every extreme that they name: adapter_storage_slot holds each of 0 to 127 once. `row_adapter_index`: within the 32 rows of one index of rep, at most 4 rows use adapters with the same adapter_storage_slot // 4, and in every such block some value of it is used by exactly 4 rows.
All inputs are finite; a program needn't handle non-finite values.
Results may differ from a plain program's by a relative error of at most 0.0085.
Values may be sent and summed in bfloat16 or wider, within the bound.
No kernel may reach another device: no remote copies, remote signals or barrier semaphores. Data moves between devices by JAX's collectives and lax.ppermute only.
A program may use at most 64 MiB of HBM per device.

v0:
```python
import math

import jax
import jax.numpy as jnp
from jax import lax
from jax.sharding import PartitionSpec as P

HEAD_WIDTH = 128


def split_up(x, dim, devices):
    lengths = x.shape
    pieces = x.reshape(*lengths[:dim], devices, lengths[dim] // devices, *lengths[dim + 1 :])
    return jnp.moveaxis(pieces, dim, 0)


def sent_and_summed(x, axis, dim):
    pieces = split_up(x, dim, lax.axis_size(axis))
    arrived = lax.all_to_all(pieces, axis, split_axis=0, concat_axis=0, tiled=True)
    return arrived.sum(axis=0)


def total_of_pieces(x, axis):
    return lax.all_gather(x, axis).sum(0)


def attend(queries, new_key_value, key_value_cache, lengths):
    row_count = queries.shape[0]
    head_count = queries.shape[1] // HEAD_WIDTH
    heads = queries.reshape(row_count, head_count, HEAD_WIDTH)
    cache_rows = key_value_cache[:, 0]
    fresh_kv = new_key_value[:, 0]
    score_scale = 1.0 / math.sqrt(HEAD_WIDTH)
    scores = (
        jnp.einsum(
            "rhd,rcd->rhc", heads, cache_rows[..., :HEAD_WIDTH], preferred_element_type=jnp.float32
        )
        * score_scale
    )
    own_score = (
        jnp.einsum(
            "rhd,rd->rh", heads, fresh_kv[:, :HEAD_WIDTH], preferred_element_type=jnp.float32
        )
        * score_scale
    )
    live_mask = (jnp.arange(cache_rows.shape[1], dtype=jnp.int32)[None, :] < lengths[:, None])[
        :, None, :
    ]
    scores = jnp.where(live_mask, scores, -1e30)
    row_max = jnp.maximum(jnp.max(scores, axis=-1), own_score)
    weights = jnp.where(live_mask, jnp.exp(scores - row_max[..., None]), 0.0)
    own_weight = jnp.exp(own_score - row_max)
    denom = jnp.sum(weights, axis=-1) + own_weight
    weights_bf = (weights / denom[..., None]).astype(jnp.bfloat16)
    own_bf = (own_weight / denom).astype(jnp.bfloat16)
    mixed_out = jnp.einsum(
        "rhc,rcd->rhd", weights_bf, cache_rows[..., HEAD_WIDTH:], preferred_element_type=jnp.float32
    )
    mixed_out = mixed_out + own_bf.astype(jnp.float32)[..., None] * fresh_kv[
        :, None, HEAD_WIDTH:
    ].astype(jnp.float32)
    return mixed_out.reshape(row_count, head_count * HEAD_WIDTH).astype(jnp.bfloat16)


def on_device(
    queries,
    new_key_value,
    key_value_cache,
    lengths,
    residual,
    output_weight,
    row_adapter_index,
    adapter_storage_slot,
    adapter_down_weight,
    adapter_up_weight,
):
    row_count = queries.shape[0]
    attention_result = attend(queries, new_key_value, key_value_cache, lengths)
    partial_out = jnp.dot(attention_result, output_weight, preferred_element_type=jnp.float32)
    plain_output = sent_and_summed(partial_out, "tp", 1)
    adapt_count = adapter_down_weight.shape[0]
    rank_width = adapter_down_weight.shape[2]
    feature_out = adapter_up_weight.shape[2]
    table_size = adapter_storage_slot.shape[0]
    matches = row_adapter_index[:, None] == jnp.arange(table_size, dtype=jnp.int32)[None, :]
    row_storage_slot = jnp.sum(jnp.where(matches, adapter_storage_slot[None, :], 0), axis=1)
    rep_count = lax.axis_size("rep")
    cap_size = max(2, 4 * row_count // rep_count)
    slot_total = rep_count * cap_size
    owner_row = row_storage_slot // adapt_count
    local_idx = row_storage_slot % adapt_count
    row_iota = jnp.arange(row_count, dtype=jnp.int32)
    earlier = (owner_row[:, None] == owner_row[None, :]) & (row_iota[:, None] > row_iota[None, :])
    place_rank = jnp.sum(earlier.astype(jnp.int32), axis=1)
    target = owner_row * cap_size + place_rank
    place = jnp.arange(slot_total, dtype=jnp.int32)[:, None] == target[None, :]
    outgoing = jnp.dot(
        place.astype(jnp.bfloat16), attention_result, preferred_element_type=jnp.float32
    ).astype(jnp.bfloat16)
    outgoing = outgoing.reshape(rep_count, cap_size, attention_result.shape[1])
    slot_tag = jnp.sum(jnp.where(place, (local_idx + 1)[None, :], 0), axis=1) - 1
    slot_tag = slot_tag.reshape(rep_count, cap_size)
    flattened_up = adapter_up_weight.reshape(adapt_count * rank_width, feature_out)
    features = lax.all_to_all(outgoing, "rep", split_axis=0, concat_axis=0, tiled=True)
    tags = lax.all_to_all(slot_tag, "rep", split_axis=0, concat_axis=0, tiled=True)
    one_hot = tags[..., None] == jnp.arange(adapt_count, dtype=jnp.int32)
    products = jnp.einsum(
        "scf,kfa->scka", features, adapter_down_weight, preferred_element_type=jnp.float32
    )
    rank_part = jnp.einsum("scka,sck->sca", products, one_hot.astype(jnp.float32))
    shrink = total_of_pieces(rank_part, "tp").astype(jnp.bfloat16)
    masked_scores = shrink[:, :, None, :] * one_hot.astype(jnp.bfloat16)[..., None]
    masked_scores = masked_scores.reshape(
        features.shape[0], features.shape[1], adapt_count * rank_width
    )
    answers = jnp.einsum(
        "scj,jd->scd", masked_scores, flattened_up, preferred_element_type=jnp.float32
    )
    returned_rows = lax.all_to_all(answers, "rep", split_axis=0, concat_axis=0, tiled=True)
    returned_flat = returned_rows.reshape(slot_total, feature_out)
    place_back = (target[:, None] == jnp.arange(slot_total, dtype=jnp.int32)[None, :]).astype(
        jnp.float32
    )
    adapter_update = jnp.dot(place_back, returned_flat, precision=lax.Precision.HIGHEST)
    return (residual.astype(jnp.float32) + plain_output + adapter_update).astype(jnp.bfloat16)


def solution(mesh):
    in_specs = (
        P("rep", "tp"),
        P("rep", "tp", None),
        P("rep", "tp", None, None),
        P("rep"),
        P("rep", "tp"),
        P("tp", None),
        P("rep"),
        P(),
        P("rep", "tp", None),
        P("rep", None, "tp"),
    )
    out_specs = P("rep", "tp")
    return jax.shard_map(
        on_device, mesh=mesh, in_specs=in_specs, out_specs=out_specs, check_vma=False
    )
```

profile of v0, /device:TPU:32, one launch (start us, length us, event | category | flops | bytes accessed | tf_op | source)
XLA Modules:
  0.0 126.3 jit_solution(9445461808215874774)
XLA Ops:
  0.0 0.0 copy-start
  0.0 0.9 select_reduce_fusion.1
  0.9 0.2 convert_reduce_fusion
  1.1 0.1 select_reduce_fusion
  1.2 0.7 sub.28
  1.9 7.3 %all-to-all-start.2 = ((s32[32,1,4]{2,1,0:T(1,128)}), s32[32,1,4]{2,1,0:T(1,128)S(1)}, u32[]{:S(2)}, u32[]{:S(2)}) async-start(s32[32,1,4]{2,1,0:T(1,128)} %bitcast.10), calls=%async_computation.2 | async-start | bytes 32768 | tf_op jit(solution)/shard_map/all_to_all | solution.py:105
  9.2 0.7 iota_compare_fusion.5
  10.0 0.7 reshape.125
  10.7 0.7 slice_bitcast_fusion
  11.4 0.1 fusion.18
  11.6 2.0 %fusion.28 = (f32[32,2]{1,0:T(8,128)S(1)}, f32[32,2,128]{2,1,0:T(2,128)S(1)}) fusion(bf16[32,2,128]{2,1,0:T(2,128)(2,1)S(1)} %reshape.125, bf16[32,128,256]{2,1,0:T(8,128)(2,1)} %bitcast.47, pred[32,128]{1,0:T(8,128)(4,1)S(1)} %iota_compare_fusion.5), kind=kOutput, calls=%fused_computation.57 | convolution fusion | flops 2121664 | bytes 1102080 | tf_op jit(solution)/shard_map/rhd,rcd->rhc/dot_general | solution.py:35
  13.5 0.2 fusion.27
  13.8 1.7 %fusion.1 = bf16[32,2,128]{2,1,0:T(2,128)(2,1)S(1)} fusion(bf16[32,128,256]{2,1,0:T(8,128)(2,1)} %bitcast.48, f32[32,128]{1,0:T(8,128)S(1)} %get-tuple-element.8, f32[32,2]{1,0:T(8,128)S(1)} %get-tuple-element.6, f32[32,2]{1,0:T(8,128)S(1)} %get-tuple-element.5, f32[32,2,128]{2,1,0:T(2,128)S(1)} %get-tuple-element.14, ...), kind=kOutput, calls=%fused_computation.7 | convolution fusion | flops 2154496 | bytes 1118976 | tf_op jit(solution)/shard_map/rhc,rcd->rhd/dot_general | solution.py:56
  15.4 0.3 convolution_convert_fusion
  15.8 3.3 %copy.40 = bf16[4096,256]{1,0:T(8,128)(2,1)S(1)} copy(bf16[4096,256]{0,1:T(8,128)(2,1)} %bitcast.39) | data formatting | bytes 4194304 | tf_op jit(solution)/shard_map/dot_general | solution.py:79
  19.0 0.0 copy-start.2
  19.1 0.6 reshape.126
  19.7 0.0 all-to-all-done.2
  19.7 7.4 %all-to-all-start.1 = ((bf16[32,4,256]{2,1,0:T(4,128)(2,1)}), bf16[32,4,256]{2,1,0:T(4,128)(2,1)S(1)}, u32[]{:S(2)}, u32[]{:S(2)}) async-start(bf16[32,4,256]{2,1,0:T(4,128)(2,1)} %reshape.126), calls=%async_computation.1 | async-start | bytes 131072 | tf_op jit(solution)/shard_map/all_to_all | solution.py:104
  27.1 0.1 copy.30
  27.2 0.2 copy.37
  27.4 7.2 %all-to-all-done.1 = bf16[32,4,256]{2,1,0:T(4,128)(2,1)S(1)} async-done(((bf16[32,4,256]{2,1,0:T(4,128)(2,1)}), bf16[32,4,256]{2,1,0:T(4,128)(2,1)S(1)}, u32[]{:S(2)}, u32[]{:S(2)}) %all-to-all-start.1) | async-done | bytes 65568 | tf_op jit(solution)/shard_map/all_to_all | solution.py:104
  34.6 0.0 copy-done
  34.6 0.2 fusion.8
  34.8 0.3 fusion.5
  35.1 39.6 %all-gather = f32[512,4,64]{2,1,0:T(4,128)S(1)} all-gather(f32[32,4,64]{2,1,0:T(4,128)S(1)} %bitcast.41), channel_id=2, replica_groups=mesh['rep'=32,'tp'=16] {'tp'}, dimensions={0}, use_global_device_ids=true | all-gather | bytes 557056 | tf_op jit(solution)/shard_map/all_gather | solution.py:24
  74.6 0.2 reduce_sum.59
  74.9 0.0 copy-done.2
  74.9 0.3 convolution_bitcast_fusion.1
  75.2 0.7 copy.32
  75.9 3.9 %all-to-all-start.3 = ((f32[32,4,256]{2,1,0:T(4,128)}), f32[32,4,256]{2,1,0:T(4,128)S(1)}, u32[]{:S(2)}, u32[]{:S(2)}) async-start(f32[32,4,256]{2,1,0:T(4,128)} %copy.32), calls=%async_computation.3 | async-start | bytes 262144 | tf_op jit(solution)/shard_map/all_to_all | solution.py:119
  79.8 0.0 copy-start.1
  79.8 1.5 %convolution_bitcast_fusion = f32[16,32,256]{2,1,0:T(8,128)} fusion(bf16[32,256,1]{1,0,2:T(8,128)(2,1)S(1)} %reshape.131, bf16[16,256,256]{2,1,0:T(8,128)(2,1)S(1)} %bitcast.37), kind=kOutput, calls=%fused_computation | convolution fusion | flops 67108864 | bytes 2637824 | tf_op jit(solution)/shard_map/dot_general | solution.py:79
  81.3 6.3 %all-to-all-done.3 = f32[32,4,256]{2,1,0:T(4,128)S(1)} async-done(((f32[32,4,256]{2,1,0:T(4,128)}), f32[32,4,256]{2,1,0:T(4,128)S(1)}, u32[]{:S(2)}, u32[]{:S(2)}) %all-to-all-start.3) | async-done | bytes 131104 | tf_op jit(solution)/shard_map/all_to_all | solution.py:119
  87.6 8.9 %all-to-all-start = ((f32[16,32,256]{2,1,0:T(8,128)}), f32[16,32,256]{2,1,0:T(8,128)S(1)}, u32[]{:S(2)}, u32[]{:S(2)}) async-start(f32[16,32,256]{2,1,0:T(8,128)} %convolution_bitcast_fusion), calls=%async_computation | async-start | bytes 1048576 | tf_op jit(solution)/shard_map/all_to_all | solution.py:19
  96.5 28.9 %all-to-all-done = f32[16,32,256]{2,1,0:T(8,128)S(1)} async-done(((f32[16,32,256]{2,1,0:T(8,128)}), f32[16,32,256]{2,1,0:T(8,128)S(1)}, u32[]{:S(2)}, u32[]{:S(2)}) %all-to-all-start) | async-done | bytes 524320 | tf_op jit(solution)/shard_map/all_to_all | solution.py:19
  125.5 0.0 copy-done.1
  125.5 0.8 fusion.2
  (10 shorter events, 0.2 us)
Async XLA Ops:
  0.0 34.6 %copy-start = (bf16[4,256,64]{1,2,0:T(8,128)(2,1)S(1)}, bf16[4,256,64]{1,2,0:T(8,128)(2,1)}, u32[]{:S(2)}) copy-start(bf16[4,256,64]{1,2,0:T(8,128)(2,1)} %param.18) | copy-start | bytes 393220
  1.9 17.8 %all-to-all-start.2 = ((s32[32,1,4]{2,1,0:T(1,128)}), s32[32,1,4]{2,1,0:T(1,128)S(1)}, u32[]{:S(2)}, u32[]{:S(2)}) async-start(s32[32,1,4]{2,1,0:T(1,128)} %bitcast.10), calls=%async_computation.2 | async-start | bytes 32768 | tf_op jit(solution)/shard_map/all_to_all | solution.py:105
  19.0 55.8 %copy-start.2 = (bf16[4,64,256]{2,1,0:T(8,128)(2,1)S(1)}, bf16[4,64,256]{2,1,0:T(8,128)(2,1)}, u32[]{:S(2)}) copy-start(bf16[4,64,256]{2,1,0:T(8,128)(2,1)} %param.19) | copy-start | bytes 393220
  19.7 14.9 %all-to-all-start.1 = ((bf16[32,4,256]{2,1,0:T(4,128)(2,1)}), bf16[32,4,256]{2,1,0:T(4,128)(2,1)S(1)}, u32[]{:S(2)}, u32[]{:S(2)}) async-start(bf16[32,4,256]{2,1,0:T(4,128)(2,1)} %reshape.126), calls=%async_computation.1 | async-start | bytes 131072 | tf_op jit(solution)/shard_map/all_to_all | solution.py:104
  75.9 11.7 %all-to-all-start.3 = ((f32[32,4,256]{2,1,0:T(4,128)}), f32[32,4,256]{2,1,0:T(4,128)S(1)}, u32[]{:S(2)}, u32[]{:S(2)}) async-start(f32[32,4,256]{2,1,0:T(4,128)} %copy.32), calls=%async_computation.3 | async-start | bytes 262144 | tf_op jit(solution)/shard_map/all_to_all | solution.py:119
  79.8 45.7 %copy-start.1 = (bf16[32,256]{1,0:T(8,128)(2,1)S(1)}, bf16[32,256]{1,0:T(8,128)(2,1)}, u32[]{:S(2)}) copy-start(bf16[32,256]{1,0:T(8,128)(2,1)} %param.14) | copy-start | bytes 49156
  87.6 37.9 %all-to-all-start = ((f32[16,32,256]{2,1,0:T(8,128)}), f32[16,32,256]{2,1,0:T(8,128)S(1)}, u32[]{:S(2)}, u32[]{:S(2)}) async-start(f32[16,32,256]{2,1,0:T(8,128)} %convolution_bitcast_fusion), calls=%async_computation | async-start | bytes 1048576 | tf_op jit(solution)/shard_map/all_to_all | solution.py:19
where the time goes:
time: 127 us; the launch traced here: 126 us
  waiting for transfers between devices  42.4 us (33%)
  blocking collectives  39.6 us (31%)
  starting transfers between devices  27.4 us (22%)
  matrix products  7.17 us (6%)
  local copies, waits for them, and re-layouts  6.48 us (5%)
  other arithmetic  3.13 us (2%)
    all_gather x1, blocking collectives, total_of_pieces(): return lax.all_gather(x, axis).sum(0)  39.6 us
    all_to_all x1, waiting for transfers between devices, sent_and_summed(): lax.all_to_all(pieces, axis, split_axis=0, concat_axis=0, tiled=True)  28.9 us
    all_to_all x1, starting transfers between devices, sent_and_summed(): lax.all_to_all(pieces, axis, split_axis=0, concat_axis=0, tiled=True)  8.88 us
    all_to_all x1, starting transfers between devices, on_device(): lax.all_to_all(outgoing, 'rep', split_axis=0, concat_axis=0, tiled=True)  7.38 us
    all_to_all x1, starting transfers between devices, on_device(): lax.all_to_all(slot_tag, 'rep', split_axis=0, concat_axis=0, tiled=True)  7.32 us
    all_to_all x1, waiting for transfers between devices, on_device(): lax.all_to_all(outgoing, 'rep', split_axis=0, concat_axis=0, tiled=True)  7.18 us
    all_to_all x1, waiting for transfers between devices, on_device(): lax.all_to_all(answers, 'rep', split_axis=0, concat_axis=0, tiled=True)  6.28 us
    all_to_all x1, starting transfers between devices, on_device(): lax.all_to_all(answers, 'rep', split_axis=0, concat_axis=0, tiled=True)  3.85 us
  transfers between devices with their start and end apart: 4, of which 3 were waited for; matrix products, arithmetic and copies ran while one was open for 10% of the time, Pallas kernels for 0%

commit v1 on v0

v1 whole, which is shorter than its diff:
```python
import functools
import math

import jax
import jax.numpy as jnp
from jax import lax
from jax.experimental import pallas as pl
from jax.experimental.pallas import tpu as pltpu
from jax.sharding import PartitionSpec as P

HEAD_WIDTH = 128
ROWS = 32
CTX = 128
REP = 32
TP = 16
CAP = 4
GROUP = 8
F32 = jnp.float32
BF16 = jnp.bfloat16
VMEM = pl.BlockSpec(memory_space=pltpu.VMEM)
ANY = pl.BlockSpec(memory_space=pl.ANY)


def iota(shape, dim):
    return lax.broadcasted_iota(jnp.int32, shape, dim)


def dot(a, b):
    return jnp.dot(a, b, preferred_element_type=F32)


def dot_t(a, b):
    return lax.dot_general(a, b, (((1,), (1,)), ((), ())), preferred_element_type=F32)


def one_hot(hit):
    return jnp.where(hit, 1.0, 0.0).astype(BF16)


def to_column(row):
    size = row.shape[1]
    eye = iota((size, size), 0) == iota((size, size), 1)
    return jnp.sum(jnp.where(eye, row, 0), axis=1, keepdims=True)


def to_row(column):
    size = column.shape[0]
    eye = iota((size, size), 0) == iota((size, size), 1)
    return jnp.sum(jnp.where(eye, column, 0), axis=0, keepdims=True)


def attend_kernel(
    q_ref, fresh_ref, lengths_ref, index_ref, table_ref, kv_hbm,
    attended_ref, send_ref, back_ref, kv_ref, sems,
):
    groups = ROWS // GROUP
    copies = [
        pltpu.make_async_copy(
            kv_hbm.at[pl.ds(g * GROUP, GROUP)], kv_ref.at[pl.ds(g * GROUP, GROUP)], sems.at[g]
        )
        for g in range(groups)
    ]
    for copy in copies:
        copy.start()

    table = table_ref[...]
    index = to_column(index_ref[...])
    size = table.shape[1]
    slot = jnp.sum(jnp.where(index == iota((ROWS, size), 1), table, 0), axis=1, keepdims=True)
    owner = slot // 4
    local = slot - owner * 4
    owner_row = to_row(owner)
    earlier = (owner == owner_row) & (iota((ROWS, ROWS), 0) > iota((ROWS, ROWS), 1))
    rank = jnp.sum(jnp.where(earlier, 1, 0), axis=1, keepdims=True)
    target = owner * CAP + rank
    back = iota((ROWS, 2 * REP * CAP), 1)
    for half in range(2):
        back_ref[half * ROWS:(half + 1) * ROWS, :] = one_hot(back == target * 2 + half)
    place = to_row(owner * 8 + rank)
    tags = one_hot(iota((ROWS, 2 * HEAD_WIDTH), 1) == local)
    rows_out = iota((8 * REP, ROWS), 0)
    place_tag = one_hot(rows_out == place + 4)
    place_row = one_hot(rows_out == place)

    lengths = to_column(lengths_ref[...])
    scale = 1.0 / math.sqrt(HEAD_WIDTH)
    row_at = iota((2 * GROUP, CTX), 0) % GROUP
    lane_at = iota((2 * GROUP, CTX), 1)
    for g in range(groups):
        at = slice(g * GROUP, (g + 1) * GROUP)
        q = q_ref[at, :].astype(F32)
        heads = jnp.concatenate([q[:, :HEAD_WIDTH], q[:, HEAD_WIDTH:]], axis=0)
        fresh = fresh_ref[at, :].astype(F32)
        fresh_key = jnp.concatenate([fresh[:, :HEAD_WIDTH]] * 2, axis=0)
        fresh_value = jnp.concatenate([fresh[:, HEAD_WIDTH:]] * 2, axis=0)
        own = jnp.sum(heads * fresh_key, axis=1, keepdims=True) * scale
        heads = heads.astype(BF16)
        live = lane_at < jnp.concatenate([lengths[at, :]] * 2, axis=0)
        copies[g].wait()
        scores = jnp.zeros((2 * GROUP, CTX), F32)
        for i in range(GROUP):
            part = dot_t(heads, kv_ref[g * GROUP + i, :, :HEAD_WIDTH])
            scores = jnp.where(row_at == i, part, scores)
        scores = jnp.where(live, scores * scale, -1e30)
        top = jnp.maximum(jnp.max(scores, axis=1, keepdims=True), own)
        weights = jnp.where(live, jnp.exp(scores - top), 0.0)
        own_weight = jnp.exp(own - top)
        denom = jnp.sum(weights, axis=1, keepdims=True) + own_weight
        probs = (weights / denom).astype(BF16)
        own_prob = (own_weight / denom).astype(BF16).astype(F32)
        mixed = jnp.zeros((2 * GROUP, HEAD_WIDTH), F32)
        for i in range(GROUP):
            part = dot(probs, kv_ref[g * GROUP + i, :, HEAD_WIDTH:])
            mixed = jnp.where(row_at == i, part, mixed)
        mixed = mixed + own_prob * fresh_value
        attended_ref[at, :] = jnp.concatenate([mixed[:GROUP], mixed[GROUP:]], axis=1).astype(BF16)
    send_ref[...] = (dot(place_row, attended_ref[...]) + dot(place_tag, tags)).astype(BF16)


def attend(queries, fresh, lengths, index, table, cache):
    return pl.pallas_call(
        attend_kernel,
        out_shape=(
            jax.ShapeDtypeStruct((ROWS, 2 * HEAD_WIDTH), BF16),
            jax.ShapeDtypeStruct((8 * REP, 2 * HEAD_WIDTH), BF16),
            jax.ShapeDtypeStruct((2 * ROWS, 2 * REP * CAP), BF16),
        ),
        in_specs=[VMEM] * 5 + [ANY],
        out_specs=(VMEM,) * 3,
        scratch_shapes=[
            pltpu.VMEM((ROWS, CTX, 2 * HEAD_WIDTH), BF16),
            pltpu.SemaphoreType.DMA((ROWS // GROUP,)),
        ],
        compiler_params=pltpu.CompilerParams(vmem_limit_bytes=16 * 2**20),
        name="attend",
    )(queries, fresh, lengths, index, table, cache)


def base_kernel(attended_ref, weight_ref, merged_ref):
    attended = attended_ref[...]
    for piece in range(TP):
        for half in range(2):
            at = (2 * piece + half) * 128
            merged_ref[piece, half * ROWS:(half + 1) * ROWS, :] = dot(
                attended, weight_ref[:, at:at + 128]
            ).astype(BF16)
        merged_ref[piece, 2 * ROWS:, :] = jnp.zeros((2 * ROWS, 128), BF16)


def base(attended, weight):
    return pl.pallas_call(
        base_kernel,
        out_shape=jax.ShapeDtypeStruct((TP, 4 * ROWS, 128), BF16),
        in_specs=[VMEM] * 2,
        out_specs=VMEM,
        compiler_params=pltpu.CompilerParams(vmem_limit_bytes=16 * 2**20),
        cost_estimate=pl.CostEstimate(
            flops=2 * 32 * 256 * 4096, bytes_accessed=3 * 2**20, transcendentals=0
        ),
        name="base",
    )(attended, weight)


def down_kernel(arrived_ref, down_ref, merged_in, merged_ref, mask_ref):
    arrived = arrived_ref[...]
    slots = REP * CAP
    slot = iota((slots, 8 * REP), 0)
    source = (slot // CAP) * 8 + slot % CAP
    at = iota((slots, 8 * REP), 1)
    features = dot(one_hot(at == source), arrived).astype(BF16)
    tags = dot(one_hot(at == source + 4), arrived[:, :128]).astype(BF16)
    spread = one_hot(iota((128, 256), 1) // 64 == iota((128, 256), 0))
    mask = dot(tags, spread)
    mask_ref[...] = mask.astype(BF16)
    product = dot_t(features, down_ref[...]) * mask
    product = product[:, :128] + product[:, 128:]
    product = product + pltpu.roll(product, 64, 1)
    low = iota((slots // 2, 128), 1) < 64
    part = jnp.where(low, product[:slots // 2], product[slots // 2:]).astype(BF16)
    for piece in range(TP):
        merged_ref[piece, 0:64, :] = merged_in[piece, 0:64, :]
        merged_ref[piece, 64:, :] = part


def down(arrived, down_weight, merged):
    return pl.pallas_call(
        down_kernel,
        out_shape=(
            jax.ShapeDtypeStruct(merged.shape, BF16),
            jax.ShapeDtypeStruct((REP * CAP, 256), BF16),
        ),
        in_specs=[VMEM] * 3,
        out_specs=(VMEM,) * 2,
        compiler_params=pltpu.CompilerParams(vmem_limit_bytes=16 * 2**20),
        name="down",
    )(arrived, down_weight, merged)


def up_kernel(merged_ref, mask_ref, up_ref, answer_ref, base_ref):
    total = merged_ref[0].astype(F32)
    for piece in range(1, TP):
        total = total + merged_ref[piece].astype(F32)
    base_ref[...] = total[:64]
    shrink = total[64:].astype(BF16).astype(F32)
    turned = pltpu.roll(shrink, 64, 1)
    low = iota(shrink.shape, 1) < 64
    shrink = jnp.concatenate(
        [jnp.where(low, shrink, turned), jnp.where(low, turned, shrink)], axis=0
    ).astype(BF16)
    spread = jnp.concatenate([shrink, shrink], axis=1) * mask_ref[...]
    answers = dot(spread, up_ref[...]).astype(BF16)
    slots = REP * CAP
    row = iota((2 * slots, slots), 0)
    at = iota((2 * slots, slots), 1)
    answer_ref[...] = (
        dot(one_hot(row == 2 * at), answers[:, :128])
        + dot(one_hot(row == 2 * at + 1), answers[:, 128:])
    ).astype(BF16)


def up(merged, mask, up_weight):
    return pl.pallas_call(
        up_kernel,
        out_shape=(
            jax.ShapeDtypeStruct((2 * REP * CAP, 128), BF16),
            jax.ShapeDtypeStruct((2 * ROWS, 128), F32),
        ),
        in_specs=[VMEM] * 3,
        out_specs=(VMEM,) * 2,
        compiler_params=pltpu.CompilerParams(vmem_limit_bytes=16 * 2**20),
        name="up",
    )(merged, mask, up_weight)


def final_kernel(returned_ref, back_ref, base_ref, residual_ref, out_ref):
    total = dot(back_ref[...], returned_ref[...]) + base_ref[...]
    total = jnp.concatenate([total[:ROWS], total[ROWS:]], axis=1)
    out_ref[...] = (residual_ref[...].astype(F32) + total).astype(BF16)


def final(returned, back, base_out, residual):
    return pl.pallas_call(
        final_kernel,
        out_shape=jax.ShapeDtypeStruct(residual.shape, BF16),
        in_specs=[VMEM] * 4,
        out_specs=VMEM,
        name="final",
    )(returned, back, base_out, residual)


def exchange(x, axis):
    return lax.all_to_all(x, axis, split_axis=0, concat_axis=0, tiled=True)


def on_device(
    queries,
    new_key_value,
    key_value_cache,
    lengths,
    residual,
    output_weight,
    row_adapter_index,
    adapter_storage_slot,
    adapter_down_weight,
    adapter_up_weight,
):
    attended, send, back = attend(
        queries,
        new_key_value.reshape(ROWS, 2 * HEAD_WIDTH),
        lengths.reshape(1, ROWS),
        row_adapter_index.reshape(1, ROWS),
        adapter_storage_slot.reshape(1, -1),
        key_value_cache.reshape(ROWS, CTX, 2 * HEAD_WIDTH),
    )
    arrived = exchange(send.reshape(REP, 8, 256), "rep").reshape(8 * REP, 256)
    merged = base(attended, output_weight)
    down_weight = jnp.swapaxes(adapter_down_weight, 1, 2).reshape(256, 256)
    merged, mask = down(arrived, down_weight, merged)
    merged = exchange(merged, "tp")
    answers, base_out = up(merged, mask, adapter_up_weight.reshape(256, 256))
    returned = exchange(answers.reshape(REP, 8, 128), "rep").reshape(8 * REP, 128)
    return final(returned, back, base_out, residual)


def solution(mesh):
    in_specs = (
        P("rep", "tp"),
        P("rep", "tp", None),
        P("rep", "tp", None, None),
        P("rep"),
        P("rep", "tp"),
        P("tp", None),
        P("rep"),
        P(),
        P("rep", "tp", None),
        P("rep", None, "tp"),
    )
    out_specs = P("rep", "tp")
    return jax.shard_map(
        on_device, mesh=mesh, in_specs=in_specs, out_specs=out_specs, check_vma=False
    )
```

time: 127 us -> 83.4 us (0.66)
  the two profiles are of different devices: /device:TPU:32 before, /device:TPU:1 now
where the time goes in v1:
time: 83.4 us; the launch traced here: 83 us
  blocking collectives  53.5 us (64%)
  starting transfers between devices  10.4 us (12%)
  waiting for transfers between devices  7.29 us (9%)
  Pallas kernels  6.58 us (8%)
  local copies, waits for them, and re-layouts  5.16 us (6%)
    all_to_all x2, blocking collectives, exchange(): return lax.all_to_all(x, axis, split_axis=0, concat_axis=0, tiled=True)  53.5 us
    all_to_all x1, starting transfers between devices, exchange(): return lax.all_to_all(x, axis, split_axis=0, concat_axis=0, tiled=True)  10.4 us
    all_to_all x1, waiting for transfers between devices, exchange(): return lax.all_to_all(x, axis, split_axis=0, concat_axis=0, tiled=True)  7.29 us
    unnamed x22, local copies, waits for them, and re-layouts  5.16 us
    pallas_call x1, Pallas kernels, attend(): pl.pallas_call(attend_kernel, out_shape=(jax.ShapeDtypeStruct((ROWS, 2 *...  3.73 us
  transfers between devices with their start and end apart: 1, of which 1 were waited for; matrix products, arithmetic and copies ran while one was open for 0% of the time, Pallas kernels for 0%

profile of v1, /device:TPU:1, one launch (start us, length us, event | category | flops | bytes accessed | tf_op | source)
XLA Modules:
  0.0 83.0 jit_solution(12756587763643028031)
XLA Ops:
  0.0 0.0 copy-start
  0.0 0.0 copy-start.1
  0.0 1.7 %copy-done.1 = bf16[32,1,128,256]{3,2,1,0:T(8,128)(2,1)S(1)} copy-done((bf16[32,1,128,256]{3,2,1,0:T(8,128)(2,1)S(1)}, bf16[32,1,128,256]{3,2,1,0:T(8,128)(2,1)}, u32[]{:S(2)}) %copy-start.1) | copy-done | bytes 2097176
  1.7 0.0 copy-start.6
  1.7 0.7 copy-done.6
  2.5 0.0 copy-start.7
  2.5 0.7 copy-done.7
  3.2 0.0 copy-start.8
  3.2 0.7 copy-done.8
  3.8 0.0 copy-start.9
  3.8 0.7 copy-done.9
  4.5 0.0 copy-start.10
  4.5 0.7 copy-done.10
  5.1 0.0 copy-start.2
  5.1 3.7 %attend.1 = (bf16[32,256]{1,0:T(8,128)(2,1)S(1)}, bf16[256,256]{1,0:T(8,128)(2,1)}, bf16[64,256]{1,0:T(8,128)(2,1)S(1)}) custom-call(bf16[32,256]{1,0:T(8,128)(2,1)S(1)} %copy-done.6, bf16[32,256]{1,0:T(8,128)(2,1)S(1)} %bitcast.18, s32[1,32]{1,0:T(1,128)S(1)} %bitcast.19, s32[1,32]{1,0:T(1,128)S(1)} %bitcast.20, s32[1,128]{1,0:T(1,128)S(1)} %bitcast.21, ...), custom_call_target="tpu_custom_call" | custom-call | tf_op jit(solution)/shard_map/attend/pallas_call | solution.py:121
  8.9 0.0 copy-start.4
  8.9 10.4 %all-to-all-start = ((bf16[32,8,256]{2,1,0:T(8,128)(2,1)}), bf16[32,8,256]{2,1,0:T(8,128)(2,1)S(1)}, u32[]{:S(2)}, u32[]{:S(2)}) async-start(bf16[32,8,256]{2,1,0:T(8,128)(2,1)} %bitcast.5), calls=%async_computation | async-start | bytes 262144 | tf_op jit(solution)/shard_map/all_to_all | solution.py:252
  19.3 0.0 copy-done.4
  19.3 0.0 copy-done
  19.3 0.0 copy-start.3
  19.3 0.4 base.1.merged_in
  19.7 7.3 %all-to-all-done = bf16[32,8,256]{2,1,0:T(8,128)(2,1)S(1)} async-done(((bf16[32,8,256]{2,1,0:T(8,128)(2,1)}), bf16[32,8,256]{2,1,0:T(8,128)(2,1)S(1)}, u32[]{:S(2)}, u32[]{:S(2)}) %all-to-all-start) | async-done | bytes 131104 | tf_op jit(solution)/shard_map/all_to_all | solution.py:252
  27.0 0.0 copy-done.2
  27.0 0.4 down.1
  27.5 35.6 %all_to_all.15.merged_ref = bf16[16,128,128]{2,1,0:T(8,128)(2,1)S(1)} all-to-all(bf16[16,128,128]{2,1,0:T(8,128)(2,1)S(1)} %get-tuple-element.14), channel_id=1, replica_groups=mesh['rep'=32,'tp'=16] {'tp'}, dimensions={0} | all-to-all | bytes 1048576 | tf_op jit(solution)/shard_map/all_to_all | solution.py:252
  63.0 0.0 copy-done.3
  63.0 0.4 up.1
  63.5 0.0 copy-start.5
  63.5 17.9 %all_to_all.16 = bf16[32,8,128]{2,1,0:T(8,128)(2,1)} all-to-all(bf16[32,8,128]{2,1,0:T(8,128)(2,1)S(1)} %bitcast.17), channel_id=1, replica_groups=mesh['rep'=32,'tp'=16] {'rep'}, dimensions={0} | all-to-all | bytes 131072 | tf_op jit(solution)/shard_map/all_to_all | solution.py:252
  81.4 0.0 copy-done.5
  81.4 1.6 %final.1 = bf16[32,256]{1,0:T(8,128)(2,1)} custom-call(bf16[256,128]{1,0:T(8,128)(2,1)} %bitcast.22, bf16[64,256]{1,0:T(8,128)(2,1)} %copy-done.4, f32[64,128]{1,0:T(8,128)} %copy-done.5, bf16[32,256]{1,0:T(8,128)(2,1)} %residual_ref.1), custom_call_target="tpu_custom_call" | custom-call | tf_op jit(solution)/shard_map/final/pallas_call | solution.py:242
Async XLA Ops:
  0.0 19.3 %copy-start = (bf16[256,4096]{1,0:T(8,128)(2,1)S(1)}, bf16[256,4096]{1,0:T(8,128)(2,1)}, u32[]{:S(2)}) copy-start(bf16[256,4096]{1,0:T(8,128)(2,1)} %weight_ref.1) | copy-start | bytes 6291460
  0.0 1.7 %copy-start.1 = (bf16[32,1,128,256]{3,2,1,0:T(8,128)(2,1)S(1)}, bf16[32,1,128,256]{3,2,1,0:T(8,128)(2,1)}, u32[]{:S(2)}) copy-start(bf16[32,1,128,256]{3,2,1,0:T(8,128)(2,1)} %param.12) | copy-start | bytes 6291460
  1.7 0.7 copy-start.6
  2.5 0.7 copy-start.7
  3.2 0.7 copy-start.8
  3.8 0.7 copy-start.9
  4.5 0.7 copy-start.10
  5.1 21.9 %copy-start.2 = (bf16[4,256,64]{1,2,0:T(8,128)(2,1)S(1)}, bf16[4,256,64]{1,2,0:T(8,128)(2,1)}, u32[]{:S(2)}) copy-start(bf16[4,256,64]{1,2,0:T(8,128)(2,1)} %param.18) | copy-start | bytes 393220
  8.9 10.4 %copy-start.4 = (bf16[64,256]{1,0:T(8,128)(2,1)}, bf16[64,256]{1,0:T(8,128)(2,1)S(1)}, u32[]{:S(2)}) copy-start(bf16[64,256]{1,0:T(8,128)(2,1)S(1)} %get-tuple-element.17.back_ref) | copy-start | bytes 98308
  8.9 18.1 %all-to-all-start = ((bf16[32,8,256]{2,1,0:T(8,128)(2,1)}), bf16[32,8,256]{2,1,0:T(8,128)(2,1)S(1)}, u32[]{:S(2)}, u32[]{:S(2)}) async-start(bf16[32,8,256]{2,1,0:T(8,128)(2,1)} %bitcast.5), calls=%async_computation | async-start | bytes 262144 | tf_op jit(solution)/shard_map/all_to_all | solution.py:252
  19.3 43.7 %copy-start.3 = (bf16[4,64,256]{2,1,0:T(8,128)(2,1)S(1)}, bf16[4,64,256]{2,1,0:T(8,128)(2,1)}, u32[]{:S(2)}) copy-start(bf16[4,64,256]{2,1,0:T(8,128)(2,1)} %param.19) | copy-start | bytes 393220
  63.5 17.9 %copy-start.5 = (f32[64,128]{1,0:T(8,128)}, f32[64,128]{1,0:T(8,128)S(1)}, u32[]{:S(2)}) copy-start(f32[64,128]{1,0:T(8,128)S(1)} %get-tuple-element.18.base_ref) | copy-start | bytes 98308

commit v2 on v1

v2 whole, which is shorter than its diff:
```python
import functools
import math

import jax
import jax.numpy as jnp
from jax import lax
from jax.experimental import pallas as pl
from jax.experimental.pallas import tpu as pltpu
from jax.sharding import Mesh
from jax.sharding import PartitionSpec as P

HEAD_WIDTH = 128
ROWS = 32
CTX = 128
REP = 32
TP = 16
CAP = 4
GROUP = 8
F32 = jnp.float32
BF16 = jnp.bfloat16
VMEM = pl.BlockSpec(memory_space=pltpu.VMEM)
HBM = pl.BlockSpec(memory_space=pltpu.HBM)


def iota(shape, dim):
    return lax.broadcasted_iota(jnp.int32, shape, dim)


def dot(a, b):
    return jnp.dot(a, b, preferred_element_type=F32)


def dot_t(a, b):
    return lax.dot_general(a, b, (((1,), (1,)), ((), ())), preferred_element_type=F32)


def one_hot(hit):
    return jnp.where(hit, 1.0, 0.0).astype(BF16)


def to_column(row):
    size = row.shape[1]
    eye = iota((size, size), 0) == iota((size, size), 1)
    return jnp.sum(jnp.where(eye, row, 0), axis=1, keepdims=True)


def to_row(column):
    size = column.shape[0]
    eye = iota((size, size), 0) == iota((size, size), 1)
    return jnp.sum(jnp.where(eye, column, 0), axis=0, keepdims=True)


def attend_kernel(
    q_hbm, fresh_hbm, lengths_hbm, index_hbm, table_hbm, kv_hbm, weight_hbm, up_hbm,
    send_ref, back_ref, kept_ref, pack_ref,
    attended_ref, q_ref, fresh_ref, lengths_ref, index_ref, table_ref, kv_ref, weight_ref, small_sems, sems, weight_sem, up_sems,
):
    groups = ROWS // GROUP
    small = [
        pltpu.make_async_copy(src, dst, small_sems.at[i])
        for i, (src, dst) in enumerate((
            (index_hbm, index_ref),
            (table_hbm, table_ref),
            (lengths_hbm, lengths_ref),
            (q_hbm, q_ref),
            (fresh_hbm, fresh_ref),
        ))
    ]
    for copy in small:
        copy.start()
    copies = [
        pltpu.make_async_copy(
            kv_hbm.at[pl.ds(g * GROUP, GROUP)], kv_ref.at[pl.ds(g * GROUP, GROUP)], sems.at[g]
        )
        for g in range(groups)
    ]
    for copy in copies:
        copy.start()
    weight_copy = pltpu.make_async_copy(weight_hbm, weight_ref, weight_sem)
    weight_copy.start()
    half_rows = TP * ROWS
    up_copies = [
        pltpu.make_async_copy(
            up_hbm.at[:, pl.ds(half * 128, 128)],
            pack_ref.at[pl.ds(half_rows + half * 256, 256)],
            up_sems.at[half],
        )
        for half in range(2)
    ]
    for copy in up_copies:
        copy.start()
    for copy in small + copies:
        copy.wait()

    table = table_ref[...]
    index = to_column(index_ref[...])
    size = table.shape[1]
    slot = jnp.sum(jnp.where(index == iota((ROWS, size), 1), table, 0), axis=1, keepdims=True)
    owner = slot // 4
    local = slot - owner * 4
    owner_row = to_row(owner)
    earlier = (owner == owner_row) & (iota((ROWS, ROWS), 0) > iota((ROWS, ROWS), 1))
    rank = jnp.sum(jnp.where(earlier, 1, 0), axis=1, keepdims=True)
    target = owner * CAP + rank
    back = iota((ROWS, 2 * REP * CAP), 1)
    for half in range(2):
        back_ref[half * ROWS:(half + 1) * ROWS, :] = one_hot(back == target * 2 + half)
    place = to_row(owner * 8 + rank)
    tags = one_hot(iota((ROWS, 2 * HEAD_WIDTH), 1) == local)
    rows_out = iota((8 * REP, ROWS), 0)
    place_tag = one_hot(rows_out == place + 4)
    place_row = one_hot(rows_out == place)

    lengths = to_column(lengths_ref[...])
    scale = 1.0 / math.sqrt(HEAD_WIDTH)
    row_at = iota((2 * GROUP, CTX), 0) % GROUP
    lane_at = iota((2 * GROUP, CTX), 1)
    for g in range(groups):
        at = slice(g * GROUP, (g + 1) * GROUP)
        q = q_ref[at, :].astype(F32)
        heads = jnp.concatenate([q[:, :HEAD_WIDTH], q[:, HEAD_WIDTH:]], axis=0)
        fresh = fresh_ref[at, :].astype(F32)
        fresh_key = jnp.concatenate([fresh[:, :HEAD_WIDTH]] * 2, axis=0)
        fresh_value = jnp.concatenate([fresh[:, HEAD_WIDTH:]] * 2, axis=0)
        own = jnp.sum(heads * fresh_key, axis=1, keepdims=True) * scale
        heads = heads.astype(BF16)
        live = lane_at < jnp.concatenate([lengths[at, :]] * 2, axis=0)
        scores = jnp.zeros((2 * GROUP, CTX), F32)
        for i in range(GROUP):
            part = dot_t(heads, kv_ref[g * GROUP + i, :, :HEAD_WIDTH])
            scores = jnp.where(row_at == i, part, scores)
        scores = jnp.where(live, scores * scale, -1e30)
        top = jnp.maximum(jnp.max(scores, axis=1, keepdims=True), own)
        weights = jnp.where(live, jnp.exp(scores - top), 0.0)
        own_weight = jnp.exp(own - top)
        denom = jnp.sum(weights, axis=1, keepdims=True) + own_weight
        probs = (weights / denom).astype(BF16)
        own_prob = (own_weight / denom).astype(BF16).astype(F32)
        mixed = jnp.zeros((2 * GROUP, HEAD_WIDTH), F32)
        for i in range(GROUP):
            part = dot(probs, kv_ref[g * GROUP + i, :, HEAD_WIDTH:])
            mixed = jnp.where(row_at == i, part, mixed)
        mixed = mixed + own_prob * fresh_value
        attended_ref[at, :] = jnp.concatenate([mixed[:GROUP], mixed[GROUP:]], axis=1).astype(BF16)
    attended = attended_ref[...]
    weight_copy.wait()
    mine = lax.axis_index("near")
    for piece in range(TP):
        for ref, half in ((pack_ref, 1 - mine), (kept_ref, mine)):
            at = pl.multiple_of((2 * piece + half) * 128, 128)
            ref[piece * ROWS:(piece + 1) * ROWS, :] = dot(
                attended, weight_ref[:, pl.ds(at, 128)]
            ).astype(BF16)
    send_ref[...] = (dot(place_row, attended_ref[...]) + dot(place_tag, tags)).astype(BF16)
    for copy in up_copies:
        copy.wait()


def attend(queries, fresh, lengths, index, table, cache, weight, up_weight):
    return pl.pallas_call(
        attend_kernel,
        out_shape=(
            jax.ShapeDtypeStruct((8 * REP, 2 * HEAD_WIDTH), BF16),
            jax.ShapeDtypeStruct((2 * ROWS, 2 * REP * CAP), BF16),
            jax.ShapeDtypeStruct((TP * ROWS, 128), BF16),
            jax.ShapeDtypeStruct((TP * ROWS + 512, 128), BF16),
        ),
        in_specs=[HBM] * 8,
        out_specs=(VMEM,) * 4,
        scratch_shapes=[
            pltpu.VMEM(queries.shape, BF16),
            pltpu.VMEM(queries.shape, BF16),
            pltpu.VMEM(fresh.shape, BF16),
            pltpu.VMEM(lengths.shape, jnp.int32),
            pltpu.VMEM(index.shape, jnp.int32),
            pltpu.VMEM(table.shape, jnp.int32),
            pltpu.VMEM((ROWS, CTX, 2 * HEAD_WIDTH), BF16),
            pltpu.VMEM(weight.shape, BF16),
            pltpu.SemaphoreType.DMA((5,)),
            pltpu.SemaphoreType.DMA((ROWS // GROUP,)),
            pltpu.SemaphoreType.DMA,
            pltpu.SemaphoreType.DMA((2,)),
        ],
        compiler_params=pltpu.CompilerParams(vmem_limit_bytes=56 * 2**20),
        name="attend",
    )(queries, fresh, lengths, index, table, cache, weight, up_weight)


def down_kernel(arrived_ref, down_ref, kept_ref, near_ref, merged_ref, mask_ref):
    arrived = arrived_ref[...]
    slots = REP * CAP
    slot = iota((slots, 8 * REP), 0)
    source = (slot % 64 // 2) * 8 + slot // 64 * 2 + slot % 2
    at = iota((slots, 8 * REP), 1)
    features = dot(one_hot(at == source), arrived).astype(BF16)
    tags = dot(one_hot(at == source + 4), arrived[:, :128]).astype(BF16)
    spread = one_hot(iota((128, 256), 1) // 64 == iota((128, 256), 0))
    mask = dot(tags, spread)
    mask_ref[...] = mask.astype(BF16)
    product = dot_t(features, down_ref[...]) * mask
    product = product[:, :128] + product[:, 128:]
    product = product + pltpu.roll(product, 64, 1)
    low = iota((32, 128), 1) < 64
    parts = [
        jnp.where(low, product[64 * p:64 * p + 32], product[64 * p + 32:64 * p + 64]).astype(BF16)
        for p in range(2)
    ]
    for piece in range(TP):
        at = slice(piece * ROWS, (piece + 1) * ROWS)
        merged_ref[piece, :ROWS, :] = (
            kept_ref[at, :].astype(F32) + near_ref[at, :].astype(F32)
        ).astype(BF16)
        merged_ref[piece, ROWS:, :] = parts[piece % 2]


def down(arrived, down_weight, kept, near):
    return pl.pallas_call(
        down_kernel,
        out_shape=(
            jax.ShapeDtypeStruct((TP, 2 * ROWS, 128), BF16),
            jax.ShapeDtypeStruct((REP * CAP, 256), BF16),
        ),
        in_specs=[VMEM] * 4,
        out_specs=(VMEM,) * 2,
        compiler_params=pltpu.CompilerParams(vmem_limit_bytes=8 * 2**20),
        name="down",
    )(arrived, down_weight, kept, near)


def up_kernel(merged_ref, mask_ref, up_ref, near_ref, answer_ref, base_ref):
    mine = lax.axis_index("near")
    sums = []
    for p in range(2):
        total = merged_ref[p].astype(F32)
        for piece in range(p + 2, TP, 2):
            total = total + merged_ref[piece].astype(F32)
        base_ref[p * ROWS:(p + 1) * ROWS, :] = total[:ROWS]
        sums.append(total[ROWS:])
    shrink = (sums[0] + sums[1]).astype(BF16).astype(F32)
    turned = pltpu.roll(shrink, 64, 1)
    low = iota(shrink.shape, 1) < 64
    shrink = jnp.concatenate(
        [jnp.where(low, shrink, turned), jnp.where(low, turned, shrink)], axis=0
    ).astype(BF16)
    mask = mask_ref[pl.ds(pl.multiple_of(mine * 64, 64), 64), :]
    spread = jnp.concatenate([shrink, shrink], axis=1) * mask
    row = iota((8 * REP, 64), 0)
    at = iota((8 * REP, 64), 1)
    first = (at // 2) * 8 + (at % 2) * 2
    total = jnp.zeros((8 * REP, 128), F32)
    for half in range(2):
        near_at = TP * ROWS + half * 256
        for up_half, side in (
            (up_ref[:, half * 128:(half + 1) * 128], mine),
            (near_ref[near_at:near_at + 256, :], 1 - mine),
        ):
            answers = dot(spread, up_half).astype(BF16)
            total = total + dot(one_hot(row == first + side * 4 + half), answers)
    answer_ref[...] = total.astype(BF16)


def up(merged, mask, up_weight, near):
    return pl.pallas_call(
        up_kernel,
        out_shape=(
            jax.ShapeDtypeStruct((8 * REP, 128), BF16),
            jax.ShapeDtypeStruct((2 * ROWS, 128), F32),
        ),
        in_specs=[VMEM] * 4,
        out_specs=(VMEM,) * 2,
        compiler_params=pltpu.CompilerParams(vmem_limit_bytes=8 * 2**20),
        name="up",
    )(merged, mask, up_weight, near)


def final_kernel(returned_ref, back_ref, base_ref, residual_ref, out_ref):
    total = dot(back_ref[...], returned_ref[...]) + base_ref[...]
    total = jnp.concatenate([total[:ROWS], total[ROWS:]], axis=1)
    out_ref[...] = (residual_ref[...].astype(F32) + total).astype(BF16)


def final(returned, back, base_out, residual):
    return pl.pallas_call(
        final_kernel,
        out_shape=jax.ShapeDtypeStruct(residual.shape, BF16),
        in_specs=[VMEM] * 4,
        out_specs=VMEM,
        compiler_params=pltpu.CompilerParams(vmem_limit_bytes=8 * 2**20),
        name="final",
    )(returned, back, base_out, residual)


def exchange(x, axis):
    return lax.all_to_all(x, axis, split_axis=0, concat_axis=0, tiled=True)


def swap_near(x):
    return lax.ppermute(x, "near", [(0, 1), (1, 0)])


def on_device(
    queries,
    new_key_value,
    key_value_cache,
    lengths,
    residual,
    output_weight,
    row_adapter_index,
    adapter_storage_slot,
    adapter_down_weight,
    adapter_up_weight,
):
    up_weight = adapter_up_weight.reshape(256, 256)
    send, back, kept, pack = attend(
        queries,
        new_key_value.reshape(ROWS, 2 * HEAD_WIDTH),
        lengths.reshape(1, ROWS),
        row_adapter_index.reshape(1, ROWS),
        adapter_storage_slot.reshape(1, -1),
        key_value_cache.reshape(ROWS, CTX, 2 * HEAD_WIDTH),
        output_weight,
        up_weight,
    )
    arrived = exchange(send.reshape(REP, 8, 256), "rep").reshape(8 * REP, 256)
    near = swap_near(pack)
    down_weight = jnp.swapaxes(adapter_down_weight, 1, 2).reshape(256, 256)
    merged, mask = down(arrived, down_weight, kept, near)
    merged = exchange(merged, ("far", "near"))
    answers, base_out = up(merged, mask, up_weight, near)
    returned = exchange(answers.reshape(2 * REP, 4, 128), ("rep", "near")).reshape(8 * REP, 128)
    return final(returned, back, base_out, residual)


def solution(mesh):
    mesh = Mesh(mesh.devices.reshape(REP, TP // 2, 2), ("rep", "far", "near"))
    tp = ("far", "near")
    in_specs = (
        P("rep", tp),
        P("rep", tp, None),
        P("rep", tp, None, None),
        P("rep"),
        P("rep", tp),
        P(tp, None),
        P("rep"),
        P(),
        P("rep", tp, None),
        P("rep", None, tp),
    )
    return jax.shard_map(
        on_device, mesh=mesh, in_specs=in_specs, out_specs=P("rep", tp), check_vma=False
    )
```

time: 83.4 us -> 74.5 us (0.89)
  blocking collectives: 53.5 us -> 61.5 us
  waiting for transfers between devices: 7.29 us -> 0.01 us
  starting transfers between devices: 10.4 us -> 4.37 us
  local copies, waits for them, and re-layouts: 5.16 us -> 0.92 us
    all_to_all x1 -> x0, starting transfers between devices: 10.4 us -> none  [exchange(): return lax.all_to_all(x, axis, split_axis=0, concat_axis=0, tiled=True)]
    all_to_all x2 -> x3, blocking collectives: 53.5 us -> 61.5 us  [exchange(): return lax.all_to_all(x, axis, split_axis=0, concat_axis=0, tiled=True)]
    all_to_all x1 -> x0, waiting for transfers between devices: 7.29 us -> none  [exchange(): return lax.all_to_all(x, axis, split_axis=0, concat_axis=0, tiled=True)]
    ppermute x0 -> x1, starting transfers between devices: none -> 4.37 us  [swap_near(): return lax.ppermute(x, 'near', [(0, 1), (1, 0)])]
    unnamed x22 -> x10, local copies, waits for them, and re-layouts: 5.16 us -> 0.92 us
    pallas_call x4 -> x3, Pallas kernels: 4.97 us -> 6.59 us  [the longest x1 5.59 us: attend(): pl.pallas_call(attend_kernel, out_shape=(jax.ShapeDtypeStruct((8 * REP, 2...]
    pallas_call x1, Pallas kernels: 1.61 us -> 0.75 us  [final(): pl.pallas_call(final_kernel, out_shape=jax.ShapeDtypeStruct(residual.shap...]
  transfers between devices with their start and end apart: 1 -> 1, of which waited for: 1 -> 0; matrix products, arithmetic and copies ran while one was open for 0% -> 0% of each run, Pallas kernels for 0% -> 0%
where the time goes in v2:
time: 74.5 us; the launch traced here: 74.1 us
  blocking collectives  61.5 us (83%)
  Pallas kernels  7.33 us (10%)
  starting transfers between devices  4.37 us (6%)
  local copies, waits for them, and re-layouts  0.92 us (1%)
    all_to_all x3, blocking collectives, exchange(): return lax.all_to_all(x, axis, split_axis=0, concat_axis=0, tiled=True)  61.5 us
    pallas_call x1, Pallas kernels, attend(): pl.pallas_call(attend_kernel, out_shape=(jax.ShapeDtypeStruct((8 * REP, 2...  5.59 us
    ppermute x1, starting transfers between devices, swap_near(): return lax.ppermute(x, 'near', [(0, 1), (1, 0)])  4.37 us
  transfers between devices with their start and end apart: 1, of which 0 were waited for; matrix products, arithmetic and copies ran while one was open for 0% of the time, Pallas kernels for 0%

profile of v2, /device:TPU:1, one launch (start us, length us, event | category | flops | bytes accessed | tf_op | source)
XLA Modules:
  0.0 74.1 jit_solution(5002302223264078252)
XLA Ops:
  0.0 0.0 copy-start.1
  0.0 0.0 copy-start
  0.0 5.6 %attend.1 = (bf16[256,256]{1,0:T(8,128)(2,1)}, bf16[64,256]{1,0:T(8,128)(2,1)}, bf16[512,128]{1,0:T(8,128)(2,1)}, bf16[1024,128]{1,0:T(8,128)(2,1)}) custom-call(bf16[32,256]{1,0:T(8,128)(2,1)} %q_hbm.1, bf16[32,256]{1,0:T(8,128)(2,1)} %bitcast.21, s32[1,32]{1,0:T(1,128)} %bitcast.22, s32[1,32]{1,0:T(1,128)} %bitcast.23, s32[1,128]{1,0:T(1,128)} %bitcast.24, ...), custom_call_target="tpu_custom_call" | custom-call | tf_op jit(solution)/shard_map/attend/pallas_call | solution.py:160
  5.6 0.0 copy-start.3
  5.6 0.0 copy-start.4
  5.6 4.4 %collective-permute-start = (bf16[1024,128]{1,0:T(8,128)(2,1)}, bf16[1024,128]{1,0:T(8,128)(2,1)S(1)}, u32[]{:S(2)}, u32[]{:S(2)}) collective-permute-start(bf16[1024,128]{1,0:T(8,128)(2,1)} %get-tuple-element.15), channel_id=1, source_target_pairs={{0,1},{1,0},{2,3},{3,2},{4,5},{5,4},{6,7},{7,6},{8,9},{9,8},{10,11... | collective-permute-start | bytes 786440 | tf_op jit(solution)/shard_map/ppermute | solution.py:298
  10.0 15.7 %all_to_all.15 = bf16[32,8,256]{2,1,0:T(8,128)(2,1)S(1)} all-to-all(bf16[32,8,256]{2,1,0:T(8,128)(2,1)} %bitcast.20), channel_id=1, replica_groups=mesh['rep'=32,'far'=8,'near'=2] {'rep'}, dimensions={0} | all-to-all | bytes 262144 | tf_op jit(solution)/shard_map/all_to_all | solution.py:294
  25.7 0.0 collective-permute-done.near_ref
  25.7 0.0 copy-done.1
  25.7 0.0 copy-start.2
  25.7 0.9 %copy-done.2 = bf16[512,128]{1,0:T(8,128)(2,1)S(1)} copy-done((bf16[512,128]{1,0:T(8,128)(2,1)S(1)}, bf16[512,128]{1,0:T(8,128)(2,1)}, u32[]{:S(2)}) %copy-start.2) | copy-done | bytes 131096
  26.6 0.4 down.1
  27.0 27.7 %all_to_all.16.merged_ref = bf16[16,64,128]{2,1,0:T(8,128)(2,1)S(1)} all-to-all(bf16[16,64,128]{2,1,0:T(8,128)(2,1)S(1)} %get-tuple-element.16), channel_id=1, replica_groups=mesh['rep'=32,'far'=8,'near'=2] {'far','near'}, dimensions={0} | all-to-all | bytes 524288 | tf_op jit(solution)/shard_map/all_to_all | solution.py:294
  54.7 0.0 copy-done
  54.7 0.6 up.1
  55.3 18.1 %all_to_all.17 = bf16[64,4,128]{2,1,0:T(4,128)(2,1)S(1)} all-to-all(bf16[64,4,128]{2,1,0:T(4,128)(2,1)S(1)} %bitcast.18), channel_id=1, replica_groups=mesh['rep'=32,'far'=8,'near'=2] {'rep','near'}, dimensions={0} | all-to-all | bytes 131072 | tf_op jit(solution)/shard_map/all_to_all | solution.py:294
  73.4 0.0 copy-done.3
  73.4 0.0 copy-done.4
  73.4 0.7 %final.1 = bf16[32,256]{1,0:T(8,128)(2,1)} custom-call(bf16[256,128]{1,0:T(8,128)(2,1)S(1)} %bitcast.16, bf16[64,256]{1,0:T(8,128)(2,1)S(1)} %copy-done.3, f32[64,128]{1,0:T(8,128)S(1)} %get-tuple-element.20.base_ref, bf16[32,256]{1,0:T(8,128)(2,1)S(1)} %copy-done.4), custom_call_target="tpu_custom_call" | custom-call | tf_op jit(solution)/shard_map/final/pallas_call | solution.py:283
Async XLA Ops:
  0.0 25.7 %copy-start.1 = (bf16[4,256,64]{1,2,0:T(8,128)(2,1)S(1)}, bf16[4,256,64]{1,2,0:T(8,128)(2,1)}, u32[]{:S(2)}) copy-start(bf16[4,256,64]{1,2,0:T(8,128)(2,1)} %param.18) | copy-start | bytes 393220
  0.0 54.7 %copy-start = (bf16[4,64,256]{2,1,0:T(8,128)(2,1)S(1)}, bf16[4,64,256]{2,1,0:T(8,128)(2,1)}, u32[]{:S(2)}) copy-start(bf16[4,64,256]{2,1,0:T(8,128)(2,1)} %param.19) | copy-start | bytes 393220
  5.6 67.8 %copy-start.3 = (bf16[64,256]{1,0:T(8,128)(2,1)S(1)}, bf16[64,256]{1,0:T(8,128)(2,1)}, u32[]{:S(2)}) copy-start(bf16[64,256]{1,0:T(8,128)(2,1)} %get-tuple-element.19.back_ref) | copy-start | bytes 98308
  5.6 67.8 %copy-start.4 = (bf16[32,256]{1,0:T(8,128)(2,1)S(1)}, bf16[32,256]{1,0:T(8,128)(2,1)}, u32[]{:S(2)}) copy-start(bf16[32,256]{1,0:T(8,128)(2,1)} %residual_ref.1) | copy-start | bytes 49156
  5.6 20.1 %collective-permute-start = (bf16[1024,128]{1,0:T(8,128)(2,1)}, bf16[1024,128]{1,0:T(8,128)(2,1)S(1)}, u32[]{:S(2)}, u32[]{:S(2)}) collective-permute-start(bf16[1024,128]{1,0:T(8,128)(2,1)} %get-tuple-element.15), channel_id=1, source_target_pairs={{0,1},{1,0},{2,3},{3,2},{4,5},{5,4},{6,7},{7,6},{8,9},{9,8},{10,11... | collective-permute-start | bytes 786440 | tf_op jit(solution)/shard_map/ppermute | solution.py:298
  25.7 0.9 %copy-start.2 = (bf16[512,128]{1,0:T(8,128)(2,1)S(1)}, bf16[512,128]{1,0:T(8,128)(2,1)}, u32[]{:S(2)}) copy-start(bf16[512,128]{1,0:T(8,128)(2,1)} %get-tuple-element.14.kept_ref) | copy-start | bytes 393220

commit v3 on v2

--- a/solution.py
+++ b/solution.py
@@ -89,7 +89,7 @@
     ]
     for copy in up_copies:
         copy.start()
-    for copy in small + copies:
+    for copy in small:
         copy.wait()
 
     table = table_ref[...]
@@ -112,36 +112,40 @@
     place_row = one_hot(rows_out == place)
 
     lengths = to_column(lengths_ref[...])
+    for copy in copies:
+        copy.wait()
     scale = 1.0 / math.sqrt(HEAD_WIDTH)
+    q = q_ref[...].astype(F32)
+    heads = jnp.concatenate([q[:, :HEAD_WIDTH], q[:, HEAD_WIDTH:]], axis=0)
+    fresh = fresh_ref[...].astype(F32)
+    fresh_key = jnp.concatenate([fresh[:, :HEAD_WIDTH]] * 2, axis=0)
+    own = jnp.sum(heads * fresh_key, axis=1, keepdims=True) * scale
+    heads = jnp.concatenate([heads, heads], axis=0).astype(BF16)
+    column = iota((CTX, 4 * ROWS), 1) % ROWS
+    turned = jnp.zeros((CTX, 4 * ROWS), F32)
+    for r in range(ROWS):
+        turned = jnp.where(column == r, dot_t(kv_ref[r, :, :HEAD_WIDTH], heads), turned)
+    live = iota((2 * ROWS, CTX), 1) < jnp.concatenate([lengths] * 2, axis=0)
+    scores = jnp.where(live, turned.T[:2 * ROWS] * scale, -1e30)
+    top = jnp.maximum(jnp.max(scores, axis=1, keepdims=True), own)
+    weights = jnp.where(live, jnp.exp(scores - top), 0.0)
+    own_weight = jnp.exp(own - top)
+    denom = jnp.sum(weights, axis=1, keepdims=True) + own_weight
+    probs = weights / denom
+    own_prob = (own_weight / denom).astype(BF16).astype(F32)
     row_at = iota((2 * GROUP, CTX), 0) % GROUP
-    lane_at = iota((2 * GROUP, CTX), 1)
     for g in range(groups):
         at = slice(g * GROUP, (g + 1) * GROUP)
-        q = q_ref[at, :].astype(F32)
-        heads = jnp.concatenate([q[:, :HEAD_WIDTH], q[:, HEAD_WIDTH:]], axis=0)
-        fresh = fresh_ref[at, :].astype(F32)
-        fresh_key = jnp.concatenate([fresh[:, :HEAD_WIDTH]] * 2, axis=0)
-        fresh_value = jnp.concatenate([fresh[:, HEAD_WIDTH:]] * 2, axis=0)
-        own = jnp.sum(heads * fresh_key, axis=1, keepdims=True) * scale
-        heads = heads.astype(BF16)
-        live = lane_at < jnp.concatenate([lengths[at, :]] * 2, axis=0)
-        scores = jnp.zeros((2 * GROUP, CTX), F32)
-        for i in range(GROUP):
-            part = dot_t(heads, kv_ref[g * GROUP + i, :, :HEAD_WIDTH])
-            scores = jnp.where(row_at == i, part, scores)
-        scores = jnp.where(live, scores * scale, -1e30)
-        top = jnp.maximum(jnp.max(scores, axis=1, keepdims=True), own)
-        weights = jnp.where(live, jnp.exp(scores - top), 0.0)
-        own_weight = jnp.exp(own - top)
-        denom = jnp.sum(weights, axis=1, keepdims=True) + own_weight
-        probs = (weights / denom).astype(BF16)
-        own_prob = (own_weight / denom).astype(BF16).astype(F32)
+        both = slice(ROWS + g * GROUP, ROWS + (g + 1) * GROUP)
+        part_probs = jnp.concatenate([probs[at], probs[both]], axis=0).astype(BF16)
         mixed = jnp.zeros((2 * GROUP, HEAD_WIDTH), F32)
         for i in range(GROUP):
-            part = dot(probs, kv_ref[g * GROUP + i, :, HEAD_WIDTH:])
+            part = dot(part_probs, kv_ref[g * GROUP + i, :, HEAD_WIDTH:])
             mixed = jnp.where(row_at == i, part, mixed)
-        mixed = mixed + own_prob * fresh_value
-        attended_ref[at, :] = jnp.concatenate([mixed[:GROUP], mixed[GROUP:]], axis=1).astype(BF16)
+        value = fresh[at, HEAD_WIDTH:]
+        attended_ref[at, :] = jnp.concatenate(
+            [mixed[:GROUP] + own_prob[at] * value, mixed[GROUP:] + own_prob[both] * value], axis=1
+        ).astype(BF16)
     attended = attended_ref[...]
     weight_copy.wait()
     mine = lax.axis_index("near")
@@ -181,9 +185,9 @@
             pltpu.SemaphoreType.DMA,
             pltpu.SemaphoreType.DMA((2,)),
         ],
-        compiler_params=pltpu.CompilerParams(vmem_limit_bytes=56 * 2**20),
+        compiler_params=pltpu.CompilerParams(vmem_limit_bytes=12 * 2**20),
         name="attend",
-    )(queries, fresh, lengths, index, table, cache, weight, up_weight)
+    )(*[pltpu.with_memory_space_constraint(x, pltpu.HBM) for x in (queries, fresh, lengths, index, table, cache, weight, up_weight)])
 
 
 def down_kernel(arrived_ref, down_ref, kept_ref, near_ref, merged_ref, mask_ref):

time: 74.5 us -> 71.9 us (0.965)
  Pallas kernels: 7.33 us -> 5.96 us
  local copies, waits for them, and re-layouts: 0.92 us -> 0.01 us
    pallas_call x1, Pallas kernels: 5.59 us -> 4.22 us  [attend(): pl.pallas_call(attend_kernel, out_shape=(jax.ShapeDtypeStruct((8 * REP, 2...]
    unnamed x10 -> x6, local copies, waits for them, and re-layouts: 0.92 us -> 0.01 us
where the time goes in v3:
time: 71.9 us; the launch traced here: 71.6 us
  blocking collectives  61.3 us (85%)
  Pallas kernels  5.96 us (8%)
  starting transfers between devices  4.36 us (6%)
    all_to_all x3, blocking collectives, exchange(): return lax.all_to_all(x, axis, split_axis=0, concat_axis=0, tiled=True)  61.3 us
    ppermute x1, starting transfers between devices, swap_near(): return lax.ppermute(x, 'near', [(0, 1), (1, 0)])  4.36 us
    pallas_call x1, Pallas kernels, attend(): pl.pallas_call(attend_kernel, out_shape=(jax.ShapeDtypeStruct((8 * REP, 2...  4.22 us
  transfers between devices with their start and end apart: 1, of which 0 were waited for; matrix products, arithmetic and copies ran while one was open for 0% of the time, Pallas kernels for 0%

profile of v3, /device:TPU:1, one launch (start us, length us, event | category | flops | bytes accessed | tf_op | source)
XLA Modules:
  0.0 71.6 jit_solution(3993225619818186071)
XLA Ops:
  0.0 0.0 copy-start.1
  0.0 0.0 copy-start
  0.0 4.2 %attend.1 = (bf16[256,256]{1,0:T(8,128)(2,1)S(1)}, bf16[64,256]{1,0:T(8,128)(2,1)S(1)}, bf16[512,128]{1,0:T(8,128)(2,1)S(1)}, bf16[1024,128]{1,0:T(8,128)(2,1)S(1)}) custom-call(bf16[32,256]{1,0:T(8,128)(2,1)} %q_hbm.1, bf16[32,256]{1,0:T(8,128)(2,1)} %bitcast.21, s32[1,32]{1,0:T(1,128)} %bitcast.22, s32[1,32]{1,0:T(1,128)} %bitcast.23, s32[1,128]{1,0:T(1,128)} %bitcast.24, ...), custom_call_target="tpu_custom_call" | custom-call | tf_op jit(solution)/shard_map/attend/pallas_call | solution.py:164
  4.2 0.0 copy-start.2
  4.2 4.4 %collective-permute-start = (bf16[1024,128]{1,0:T(8,128)(2,1)S(1)}, bf16[1024,128]{1,0:T(8,128)(2,1)S(1)}, u32[]{:S(2)}, u32[]{:S(2)}) collective-permute-start(bf16[1024,128]{1,0:T(8,128)(2,1)S(1)} %get-tuple-element.15), channel_id=1, source_target_pairs={{0,1},{1,0},{2,3},{3,2},{4,5},{5,4},{6,7},{7,6},{8,9},{9,8},{10,11... | collective-permute-start | bytes 786440 | tf_op jit(solution)/shard_map/ppermute | solution.py:302
  8.6 15.5 %all_to_all.15 = bf16[32,8,256]{2,1,0:T(8,128)(2,1)S(1)} all-to-all(bf16[32,8,256]{2,1,0:T(8,128)(2,1)S(1)} %bitcast.18), channel_id=1, replica_groups=mesh['rep'=32,'far'=8,'near'=2] {'rep'}, dimensions={0} | all-to-all | bytes 262144 | tf_op jit(solution)/shard_map/all_to_all | solution.py:298
  24.1 0.0 collective-permute-done.near_ref
  24.1 0.0 copy-done.1
  24.1 0.4 down.1
  24.5 27.7 %all_to_all.16.merged_ref = bf16[16,64,128]{2,1,0:T(8,128)(2,1)S(1)} all-to-all(bf16[16,64,128]{2,1,0:T(8,128)(2,1)S(1)} %get-tuple-element.16), channel_id=1, replica_groups=mesh['rep'=32,'far'=8,'near'=2] {'far','near'}, dimensions={0} | all-to-all | bytes 524288 | tf_op jit(solution)/shard_map/all_to_all | solution.py:298
  52.2 0.0 copy-done
  52.2 0.6 up.1
  52.8 18.1 %all_to_all.17 = bf16[64,4,128]{2,1,0:T(4,128)(2,1)S(1)} all-to-all(bf16[64,4,128]{2,1,0:T(4,128)(2,1)S(1)} %bitcast.19), channel_id=1, replica_groups=mesh['rep'=32,'far'=8,'near'=2] {'rep','near'}, dimensions={0} | all-to-all | bytes 131072 | tf_op jit(solution)/shard_map/all_to_all | solution.py:298
  70.9 0.0 copy-done.2
  70.9 0.7 %final.1 = bf16[32,256]{1,0:T(8,128)(2,1)} custom-call(bf16[256,128]{1,0:T(8,128)(2,1)S(1)} %bitcast.16, bf16[64,256]{1,0:T(8,128)(2,1)S(1)} %get-tuple-element.19.back_ref, f32[64,128]{1,0:T(8,128)S(1)} %get-tuple-element.20.base_ref, bf16[32,256]{1,0:T(8,128)(2,1)S(1)} %copy-done.2), custom_call_target="tpu_custom_call" | custom-call | tf_op jit(solution)/shard_map/final/pallas_call | solution.py:287
Async XLA Ops:
  0.0 24.1 %copy-start.1 = (bf16[4,256,64]{1,2,0:T(8,128)(2,1)S(1)}, bf16[4,256,64]{1,2,0:T(8,128)(2,1)}, u32[]{:S(2)}) copy-start(bf16[4,256,64]{1,2,0:T(8,128)(2,1)} %param.18) | copy-start | bytes 393220
  0.0 52.2 %copy-start = (bf16[4,64,256]{2,1,0:T(8,128)(2,1)S(1)}, bf16[4,64,256]{2,1,0:T(8,128)(2,1)}, u32[]{:S(2)}) copy-start(bf16[4,64,256]{2,1,0:T(8,128)(2,1)} %param.19) | copy-start | bytes 393220
  4.2 66.7 %copy-start.2 = (bf16[32,256]{1,0:T(8,128)(2,1)S(1)}, bf16[32,256]{1,0:T(8,128)(2,1)}, u32[]{:S(2)}) copy-start(bf16[32,256]{1,0:T(8,128)(2,1)} %residual_ref.1) | copy-start | bytes 49156
  4.2 19.9 %collective-permute-start = (bf16[1024,128]{1,0:T(8,128)(2,1)S(1)}, bf16[1024,128]{1,0:T(8,128)(2,1)S(1)}, u32[]{:S(2)}, u32[]{:S(2)}) collective-permute-start(bf16[1024,128]{1,0:T(8,128)(2,1)S(1)} %get-tuple-element.15), channel_id=1, source_target_pairs={{0,1},{1,0},{2,3},{3,2},{4,5},{5,4},{6,7},{7,6},{8,9},{9,8},{10,11... | collective-permute-start | bytes 786440 | tf_op jit(solution)/shard_map/ppermute | solution.py:302

commit v4 on v3

--- a/solution.py
+++ b/solution.py
@@ -120,13 +120,23 @@
     fresh = fresh_ref[...].astype(F32)
     fresh_key = jnp.concatenate([fresh[:, :HEAD_WIDTH]] * 2, axis=0)
     own = jnp.sum(heads * fresh_key, axis=1, keepdims=True) * scale
-    heads = jnp.concatenate([heads, heads], axis=0).astype(BF16)
-    column = iota((CTX, 4 * ROWS), 1) % ROWS
+    empty = jnp.zeros_like(heads)
+    heads = jnp.concatenate(
+        [jnp.concatenate([heads, empty], axis=1), jnp.concatenate([empty, heads], axis=1)], axis=0
+    ).astype(BF16)
+    column = iota((CTX, 4 * ROWS), 1)
+    column = column % ROWS - column // (2 * ROWS) * (ROWS // 2)
     turned = jnp.zeros((CTX, 4 * ROWS), F32)
-    for r in range(ROWS):
-        turned = jnp.where(column == r, dot_t(kv_ref[r, :, :HEAD_WIDTH], heads), turned)
+    for r in range(ROWS // 2):
+        keys = jnp.concatenate(
+            [kv_ref[r, :, :HEAD_WIDTH], kv_ref[r + ROWS // 2, :, :HEAD_WIDTH]], axis=1
+        )
+        turned = jnp.where(column == r, dot_t(keys, heads), turned)
+    turned = turned.T
+    early = iota((2 * ROWS, CTX), 0) % ROWS < ROWS // 2
+    turned = jnp.where(early, turned[:2 * ROWS], turned[2 * ROWS:])
     live = iota((2 * ROWS, CTX), 1) < jnp.concatenate([lengths] * 2, axis=0)
-    scores = jnp.where(live, turned.T[:2 * ROWS] * scale, -1e30)
+    scores = jnp.where(live, turned * scale, -1e30)
     top = jnp.maximum(jnp.max(scores, axis=1, keepdims=True), own)
     weights = jnp.where(live, jnp.exp(scores - top), 0.0)
     own_weight = jnp.exp(own - top)
@@ -137,11 +147,12 @@
     for g in range(groups):
         at = slice(g * GROUP, (g + 1) * GROUP)
         both = slice(ROWS + g * GROUP, ROWS + (g + 1) * GROUP)
-        part_probs = jnp.concatenate([probs[at], probs[both]], axis=0).astype(BF16)
-        mixed = jnp.zeros((2 * GROUP, HEAD_WIDTH), F32)
-        for i in range(GROUP):
-            part = dot(part_probs, kv_ref[g * GROUP + i, :, HEAD_WIDTH:])
-            mixed = jnp.where(row_at == i, part, mixed)
+        part_probs = jnp.concatenate([probs[at], probs[both]], axis=0)
+        spread = jnp.concatenate(
+            [jnp.where(row_at == i, part_probs, 0.0) for i in range(GROUP)], axis=1
+        ).astype(BF16)
+        values = kv_ref[g * GROUP:(g + 1) * GROUP, :, HEAD_WIDTH:].reshape(GROUP * CTX, HEAD_WIDTH)
+        mixed = dot(spread, values)
         value = fresh[at, HEAD_WIDTH:]
         attended_ref[at, :] = jnp.concatenate(
             [mixed[:GROUP] + own_prob[at] * value, mixed[GROUP:] + own_prob[both] * value], axis=1

time: 71.9 us -> 71.3 us (level)
  no operation moved by 1% of the time
where the time goes in v4:
time: 71.3 us; the launch traced here: 71.1 us
  blocking collectives  61.3 us (86%)
  Pallas kernels  5.38 us (8%)
  starting transfers between devices  4.38 us (6%)
    all_to_all x3, blocking collectives, exchange(): return lax.all_to_all(x, axis, split_axis=0, concat_axis=0, tiled=True)  61.3 us
    ppermute x1, starting transfers between devices, swap_near(): return lax.ppermute(x, 'near', [(0, 1), (1, 0)])  4.38 us
    pallas_call x1, Pallas kernels, attend(): pl.pallas_call(attend_kernel, out_shape=(jax.ShapeDtypeStruct((8 * REP, 2...  3.64 us
  transfers between devices with their start and end apart: 1, of which 0 were waited for; matrix products, arithmetic and copies ran while one was open for 0% of the time, Pallas kernels for 0%

profile of v4, /device:TPU:1, one launch (start us, length us, event | category | flops | bytes accessed | tf_op | source)
XLA Modules:
  0.0 71.1 jit_solution(13208419894247011376)
XLA Ops:
  0.0 0.0 copy-start.1
  0.0 0.0 copy-start
  0.0 3.6 %attend.1 = (bf16[256,256]{1,0:T(8,128)(2,1)S(1)}, bf16[64,256]{1,0:T(8,128)(2,1)S(1)}, bf16[512,128]{1,0:T(8,128)(2,1)S(1)}, bf16[1024,128]{1,0:T(8,128)(2,1)S(1)}) custom-call(bf16[32,256]{1,0:T(8,128)(2,1)} %q_hbm.1, bf16[32,256]{1,0:T(8,128)(2,1)} %bitcast.21, s32[1,32]{1,0:T(1,128)} %bitcast.22, s32[1,32]{1,0:T(1,128)} %bitcast.23, s32[1,128]{1,0:T(1,128)} %bitcast.24, ...), custom_call_target="tpu_custom_call" | custom-call | tf_op jit(solution)/shard_map/attend/pallas_call | solution.py:175
  3.7 0.0 copy-start.2
  3.7 4.4 %collective-permute-start = (bf16[1024,128]{1,0:T(8,128)(2,1)S(1)}, bf16[1024,128]{1,0:T(8,128)(2,1)S(1)}, u32[]{:S(2)}, u32[]{:S(2)}) collective-permute-start(bf16[1024,128]{1,0:T(8,128)(2,1)S(1)} %get-tuple-element.15), channel_id=1, source_target_pairs={{0,1},{1,0},{2,3},{3,2},{4,5},{5,4},{6,7},{7,6},{8,9},{9,8},{10,11... | collective-permute-start | bytes 786440 | tf_op jit(solution)/shard_map/ppermute | solution.py:313
  8.1 15.5 %all_to_all.15 = bf16[32,8,256]{2,1,0:T(8,128)(2,1)S(1)} all-to-all(bf16[32,8,256]{2,1,0:T(8,128)(2,1)S(1)} %bitcast.18), channel_id=1, replica_groups=mesh['rep'=32,'far'=8,'near'=2] {'rep'}, dimensions={0} | all-to-all | bytes 262144 | tf_op jit(solution)/shard_map/all_to_all | solution.py:309
  23.5 0.0 collective-permute-done.near_ref
  23.5 0.0 copy-done.1
  23.5 0.4 down.1
  23.9 27.7 %all_to_all.16.merged_ref = bf16[16,64,128]{2,1,0:T(8,128)(2,1)S(1)} all-to-all(bf16[16,64,128]{2,1,0:T(8,128)(2,1)S(1)} %get-tuple-element.16), channel_id=1, replica_groups=mesh['rep'=32,'far'=8,'near'=2] {'far','near'}, dimensions={0} | all-to-all | bytes 524288 | tf_op jit(solution)/shard_map/all_to_all | solution.py:309
  51.6 0.0 copy-done
  51.6 0.6 up.1
  52.2 18.1 %all_to_all.17 = bf16[64,4,128]{2,1,0:T(4,128)(2,1)S(1)} all-to-all(bf16[64,4,128]{2,1,0:T(4,128)(2,1)S(1)} %bitcast.19), channel_id=1, replica_groups=mesh['rep'=32,'far'=8,'near'=2] {'rep','near'}, dimensions={0} | all-to-all | bytes 131072 | tf_op jit(solution)/shard_map/all_to_all | solution.py:309
  70.3 0.0 copy-done.2
  70.3 0.7 %final.1 = bf16[32,256]{1,0:T(8,128)(2,1)} custom-call(bf16[256,128]{1,0:T(8,128)(2,1)S(1)} %bitcast.16, bf16[64,256]{1,0:T(8,128)(2,1)S(1)} %get-tuple-element.19.back_ref, f32[64,128]{1,0:T(8,128)S(1)} %get-tuple-element.20.base_ref, bf16[32,256]{1,0:T(8,128)(2,1)S(1)} %copy-done.2), custom_call_target="tpu_custom_call" | custom-call | tf_op jit(solution)/shard_map/final/pallas_call | solution.py:298
Async XLA Ops:
  0.0 23.5 %copy-start.1 = (bf16[4,256,64]{1,2,0:T(8,128)(2,1)S(1)}, bf16[4,256,64]{1,2,0:T(8,128)(2,1)}, u32[]{:S(2)}) copy-start(bf16[4,256,64]{1,2,0:T(8,128)(2,1)} %param.18) | copy-start | bytes 393220
  0.0 51.6 %copy-start = (bf16[4,64,256]{2,1,0:T(8,128)(2,1)S(1)}, bf16[4,64,256]{2,1,0:T(8,128)(2,1)}, u32[]{:S(2)}) copy-start(bf16[4,64,256]{2,1,0:T(8,128)(2,1)} %param.19) | copy-start | bytes 393220
  3.7 66.7 %copy-start.2 = (bf16[32,256]{1,0:T(8,128)(2,1)S(1)}, bf16[32,256]{1,0:T(8,128)(2,1)}, u32[]{:S(2)}) copy-start(bf16[32,256]{1,0:T(8,128)(2,1)} %residual_ref.1) | copy-start | bytes 49156
  3.7 19.9 %collective-permute-start = (bf16[1024,128]{1,0:T(8,128)(2,1)S(1)}, bf16[1024,128]{1,0:T(8,128)(2,1)S(1)}, u32[]{:S(2)}, u32[]{:S(2)}) collective-permute-start(bf16[1024,128]{1,0:T(8,128)(2,1)S(1)} %get-tuple-element.15), channel_id=1, source_target_pairs={{0,1},{1,0},{2,3},{3,2},{4,5},{5,4},{6,7},{7,6},{8,9},{9,8},{10,11... | collective-permute-start | bytes 786440 | tf_op jit(solution)/shard_map/ppermute | solution.py:313

commit v5 on v4

--- a/solution.py
+++ b/solution.py
@@ -70,9 +70,11 @@
         copy.start()
     copies = [
         pltpu.make_async_copy(
-            kv_hbm.at[pl.ds(g * GROUP, GROUP)], kv_ref.at[pl.ds(g * GROUP, GROUP)], sems.at[g]
+            kv_hbm.at[pl.ds(g % 2 * 16, 16), :, pl.ds(g // 2 * HEAD_WIDTH, HEAD_WIDTH)],
+            kv_ref.at[pl.ds(g % 2 * 16, 16), :, pl.ds(g // 2 * HEAD_WIDTH, HEAD_WIDTH)],
+            sems.at[g],
         )
-        for g in range(groups)
+        for g in range(4)
     ]
     for copy in copies:
         copy.start()
@@ -112,7 +114,7 @@
     place_row = one_hot(rows_out == place)
 
     lengths = to_column(lengths_ref[...])
-    for copy in copies:
+    for copy in copies[:2]:
         copy.wait()
     scale = 1.0 / math.sqrt(HEAD_WIDTH)
     q = q_ref[...].astype(F32)
@@ -143,6 +145,8 @@
     denom = jnp.sum(weights, axis=1, keepdims=True) + own_weight
     probs = weights / denom
     own_prob = (own_weight / denom).astype(BF16).astype(F32)
+    for copy in copies[2:]:
+        copy.wait()
     row_at = iota((2 * GROUP, CTX), 0) % GROUP
     for g in range(groups):
         at = slice(g * GROUP, (g + 1) * GROUP)
@@ -156,8 +160,8 @@
         value = fresh[at, HEAD_WIDTH:]
         attended_ref[at, :] = jnp.concatenate(
             [mixed[:GROUP] + own_prob[at] * value, mixed[GROUP:] + own_prob[both] * value], axis=1
-        ).astype(BF16)
-    attended = attended_ref[...]
+        )
+    attended = attended_ref[...].astype(BF16)
     weight_copy.wait()
     mine = lax.axis_index("near")
     for piece in range(TP):
@@ -166,7 +170,7 @@
             ref[piece * ROWS:(piece + 1) * ROWS, :] = dot(
                 attended, weight_ref[:, pl.ds(at, 128)]
             ).astype(BF16)
-    send_ref[...] = (dot(place_row, attended_ref[...]) + dot(place_tag, tags)).astype(BF16)
+    send_ref[...] = (dot(place_row, attended) + dot(place_tag, tags)).astype(BF16)
     for copy in up_copies:
         copy.wait()
 
@@ -183,7 +187,7 @@
         in_specs=[HBM] * 8,
         out_specs=(VMEM,) * 4,
         scratch_shapes=[
-            pltpu.VMEM(queries.shape, BF16),
+            pltpu.VMEM(queries.shape, F32),
             pltpu.VMEM(queries.shape, BF16),
             pltpu.VMEM(fresh.shape, BF16),
             pltpu.VMEM(lengths.shape, jnp.int32),
@@ -192,7 +196,7 @@
             pltpu.VMEM((ROWS, CTX, 2 * HEAD_WIDTH), BF16),
             pltpu.VMEM(weight.shape, BF16),
             pltpu.SemaphoreType.DMA((5,)),
-            pltpu.SemaphoreType.DMA((ROWS // GROUP,)),
+            pltpu.SemaphoreType.DMA((4,)),
             pltpu.SemaphoreType.DMA,
             pltpu.SemaphoreType.DMA((2,)),
         ],

time: 71.3 us -> 71.3 us (level)
  no operation moved by 1% of the time
where the time goes in v5:
time: 71.3 us; the launch traced here: 71 us
  blocking collectives  61.3 us (86%)
  Pallas kernels  5.36 us (8%)
  starting transfers between devices  4.37 us (6%)
    all_to_all x3, blocking collectives, exchange(): return lax.all_to_all(x, axis, split_axis=0, concat_axis=0, tiled=True)  61.3 us
    ppermute x1, starting transfers between devices, swap_near(): return lax.ppermute(x, 'near', [(0, 1), (1, 0)])  4.37 us
    pallas_call x1, Pallas kernels, attend(): pl.pallas_call(attend_kernel, out_shape=(jax.ShapeDtypeStruct((8 * REP, 2...  3.62 us
  transfers between devices with their start and end apart: 1, of which 0 were waited for; matrix products, arithmetic and copies ran while one was open for 0% of the time, Pallas kernels for 0%

profile of v5, /device:TPU:1, one launch (start us, length us, event | category | flops | bytes accessed | tf_op | source)
XLA Modules:
  0.0 71.0 jit_solution(10012260260462688657)
XLA Ops:
  0.0 0.0 copy-start.1
  0.0 0.0 copy-start
  0.0 3.6 %attend.1 = (bf16[256,256]{1,0:T(8,128)(2,1)S(1)}, bf16[64,256]{1,0:T(8,128)(2,1)S(1)}, bf16[512,128]{1,0:T(8,128)(2,1)S(1)}, bf16[1024,128]{1,0:T(8,128)(2,1)S(1)}) custom-call(bf16[32,256]{1,0:T(8,128)(2,1)} %q_hbm.1, bf16[32,256]{1,0:T(8,128)(2,1)} %bitcast.21, s32[1,32]{1,0:T(1,128)} %bitcast.22, s32[1,32]{1,0:T(1,128)} %bitcast.23, s32[1,128]{1,0:T(1,128)} %bitcast.24, ...), custom_call_target="tpu_custom_call" | custom-call | tf_op jit(solution)/shard_map/attend/pallas_call | solution.py:179
  3.6 0.0 copy-start.2
  3.6 4.4 %collective-permute-start = (bf16[1024,128]{1,0:T(8,128)(2,1)S(1)}, bf16[1024,128]{1,0:T(8,128)(2,1)S(1)}, u32[]{:S(2)}, u32[]{:S(2)}) collective-permute-start(bf16[1024,128]{1,0:T(8,128)(2,1)S(1)} %get-tuple-element.15), channel_id=1, source_target_pairs={{0,1},{1,0},{2,3},{3,2},{4,5},{5,4},{6,7},{7,6},{8,9},{9,8},{10,11... | collective-permute-start | bytes 786440 | tf_op jit(solution)/shard_map/ppermute | solution.py:317
  8.0 15.5 %all_to_all.15 = bf16[32,8,256]{2,1,0:T(8,128)(2,1)S(1)} all-to-all(bf16[32,8,256]{2,1,0:T(8,128)(2,1)S(1)} %bitcast.18), channel_id=1, replica_groups=mesh['rep'=32,'far'=8,'near'=2] {'rep'}, dimensions={0} | all-to-all | bytes 262144 | tf_op jit(solution)/shard_map/all_to_all | solution.py:313
  23.5 0.0 collective-permute-done.near_ref
  23.5 0.0 copy-done.1
  23.5 0.4 down.1
  23.9 27.7 %all_to_all.16.merged_ref = bf16[16,64,128]{2,1,0:T(8,128)(2,1)S(1)} all-to-all(bf16[16,64,128]{2,1,0:T(8,128)(2,1)S(1)} %get-tuple-element.16), channel_id=1, replica_groups=mesh['rep'=32,'far'=8,'near'=2] {'far','near'}, dimensions={0} | all-to-all | bytes 524288 | tf_op jit(solution)/shard_map/all_to_all | solution.py:313
  51.6 0.0 copy-done
  51.6 0.6 up.1
  52.2 18.1 %all_to_all.17 = bf16[64,4,128]{2,1,0:T(4,128)(2,1)S(1)} all-to-all(bf16[64,4,128]{2,1,0:T(4,128)(2,1)S(1)} %bitcast.19), channel_id=1, replica_groups=mesh['rep'=32,'far'=8,'near'=2] {'rep','near'}, dimensions={0} | all-to-all | bytes 131072 | tf_op jit(solution)/shard_map/all_to_all | solution.py:313
  70.3 0.0 copy-done.2
  70.3 0.7 %final.1 = bf16[32,256]{1,0:T(8,128)(2,1)} custom-call(bf16[256,128]{1,0:T(8,128)(2,1)S(1)} %bitcast.16, bf16[64,256]{1,0:T(8,128)(2,1)S(1)} %get-tuple-element.19.back_ref, f32[64,128]{1,0:T(8,128)S(1)} %get-tuple-element.20.base_ref, bf16[32,256]{1,0:T(8,128)(2,1)S(1)} %copy-done.2), custom_call_target="tpu_custom_call" | custom-call | tf_op jit(solution)/shard_map/final/pallas_call | solution.py:302
Async XLA Ops:
  0.0 23.5 %copy-start.1 = (bf16[4,256,64]{1,2,0:T(8,128)(2,1)S(1)}, bf16[4,256,64]{1,2,0:T(8,128)(2,1)}, u32[]{:S(2)}) copy-start(bf16[4,256,64]{1,2,0:T(8,128)(2,1)} %param.18) | copy-start | bytes 393220
  0.0 51.6 %copy-start = (bf16[4,64,256]{2,1,0:T(8,128)(2,1)S(1)}, bf16[4,64,256]{2,1,0:T(8,128)(2,1)}, u32[]{:S(2)}) copy-start(bf16[4,64,256]{2,1,0:T(8,128)(2,1)} %param.19) | copy-start | bytes 393220
  3.6 66.7 %copy-start.2 = (bf16[32,256]{1,0:T(8,128)(2,1)S(1)}, bf16[32,256]{1,0:T(8,128)(2,1)}, u32[]{:S(2)}) copy-start(bf16[32,256]{1,0:T(8,128)(2,1)} %residual_ref.1) | copy-start | bytes 49156
  3.6 19.9 %collective-permute-start = (bf16[1024,128]{1,0:T(8,128)(2,1)S(1)}, bf16[1024,128]{1,0:T(8,128)(2,1)S(1)}, u32[]{:S(2)}, u32[]{:S(2)}) collective-permute-start(bf16[1024,128]{1,0:T(8,128)(2,1)S(1)} %get-tuple-element.15), channel_id=1, source_target_pairs={{0,1},{1,0},{2,3},{3,2},{4,5},{5,4},{6,7},{7,6},{8,9},{9,8},{10,11... | collective-permute-start | bytes 786440 | tf_op jit(solution)/shard_map/ppermute | solution.py:317
